TPU v7x, 32 devices: a whole 2x2x4 slice. The times are simulated.
32 devices in a mesh: dp: 4 (over x, core), seq: 8 (over z, y).
Axes of the slice: x: 2, y: 2, z: 4, core: 2. Of those that a mesh axis runs over, the one named last changes fastest.
Arguments:
- inputs: bfloat16 [4, 4096, 768], P('dp', 'seq'), may hold values from -6 to 6
- block_mix: bfloat16 [8, 512, 512], P('seq'), may hold values from -0.25 to 0.25
- cross_mix: bfloat16 [512, 8, 8], P('seq'), may hold values from -2 to 2
- cotangent: bfloat16 [4, 4096, 768], P('dp', 'seq'), may hold values from -0.59765625 to 0.59765625
Outputs:
- output: bfloat16 [4, 4096, 768], P('dp', 'seq')
- input_grad: bfloat16 [4, 4096, 768], P('dp', 'seq')
- block_grad: bfloat16 [8, 512, 512], P('seq')
- cross_grad: bfloat16 [512, 8, 8], P('seq')
All inputs are finite; a program needn't handle non-finite values.
Results may differ from a plain program's by a relative error of at most 0.012.
Values may be sent and summed in bfloat16 or wider, within the bound.
A program may use at most 64 MiB of HBM per device.

v0:
```python
import jax
import jax.numpy as jnp
from jax import lax
from jax.sharding import PartitionSpec as P


def local(inputs, block_mix, cross_mix, cotangent):
    h = jnp.einsum("bsr,brc->bsc", block_mix, inputs, preferred_element_type=jnp.float32).astype(
        jnp.bfloat16
    )
    gate = jax.nn.sigmoid(inputs.astype(jnp.float32))
    h_cols = lax.all_to_all(h, "seq", split_axis=1, concat_axis=0, tiled=True)
    z_cols = jnp.einsum(
        "rab,brc->arc", cross_mix, h_cols, preferred_element_type=jnp.float32
    ).astype(jnp.bfloat16)
    z = lax.all_to_all(z_cols, "seq", split_axis=0, concat_axis=1, tiled=True)
    dz = (cotangent.astype(jnp.float32) * gate).astype(jnp.bfloat16)
    dz_cols = lax.all_to_all(dz, "seq", split_axis=1, concat_axis=0, tiled=True)
    dh_cols = jnp.einsum(
        "rab,arc->brc", cross_mix, dz_cols, preferred_element_type=jnp.float32
    ).astype(jnp.bfloat16)
    cross_part = jnp.einsum("arc,brc->rab", dz_cols, h_cols, preferred_element_type=jnp.float32)
    dh = lax.all_to_all(dh_cols, "seq", split_axis=0, concat_axis=1, tiled=True)
    dv = jnp.einsum("bsr,bsc->brc", block_mix, dh, preferred_element_type=jnp.float32)
    block_part = jnp.einsum("bsc,brc->bsr", dh, inputs, preferred_element_type=jnp.float32)
    block_sum, cross_sum = (
        lax.psum(block_part.astype(jnp.bfloat16), "dp").astype(jnp.float32),
        lax.psum(cross_part.astype(jnp.bfloat16), "dp").astype(jnp.float32),
    )
    zf = z.astype(jnp.float32)
    output = (inputs.astype(jnp.float32) + zf * gate).astype(jnp.bfloat16)
    input_grad = (cotangent.astype(jnp.float32) * (1.0 + zf * gate * (1.0 - gate)) + dv).astype(
        jnp.bfloat16
    )
    return (output, input_grad, block_sum.astype(jnp.bfloat16), cross_sum.astype(jnp.bfloat16))


def solution(mesh):
    placed = (
        P("dp", "seq", None),
        P("seq", None, None),
        P("seq", None, None),
        P("dp", "seq", None),
    )
    return jax.shard_map(
        local,
        mesh=mesh,
        in_specs=placed,
        out_specs=(
            P("dp", "seq", None),
            P("dp", "seq", None),
            P("seq", None, None),
            P("seq", None, None),
        ),
        check_vma=False,
    )
```

profile of v0, /device:TPU:0, one launch (start us, length us, event | category | flops | bytes accessed | tf_op | source)
XLA Modules:
  0.0 190.0 jit_solution(17759699037681168629)
XLA Ops:
  7.2 0.0 copy-start
  7.2 1.0 copy-done
  8.2 1.7 fusion.9
  9.9 1.2 copy.73
  11.1 0.5 broadcast.12
  11.7 5.4 %reduce = bf16[512,768]{1,0:T(8,128)(2,1)S(1)} reduce(bf16[512,1,768]{2,1,0:T(2,128)(2,1)S(1)} %bitcast.39, bf16[]{:T(256)} %broadcast.12), dimensions={1}, to_apply=%bitcast.37.reduce_sub_computation | reduce | bytes 1572866
  17.1 0.0 copy-start.8
  17.1 1.1 reshape.57
  18.2 7.3 %all-to-all-start = ((bf16[8,2,24576]{2,1,0:T(2,128)(2,1)}), bf16[8,2,24576]{2,1,0:T(2,128)(2,1)S(1)}, u32[]{:S(2)}, u32[]{:S(2)}) async-start(bf16[8,2,24576]{2,1,0:T(2,128)(2,1)} %reshape.57), calls=%async_computation | async-start | bytes 1572864 | tf_op jit(solution)/shard_map/all_to_all | solution.py:12
  25.4 0.1 copy.55
  25.6 20.0 %all-to-all-done = bf16[8,2,24576]{2,1,0:T(2,128)(2,1)S(1)} async-done(((bf16[8,2,24576]{2,1,0:T(2,128)(2,1)}), bf16[8,2,24576]{2,1,0:T(2,128)(2,1)S(1)}, u32[]{:S(2)}, u32[]{:S(2)}) %all-to-all-start) | async-done | bytes 786464 | tf_op jit(solution)/shard_map/all_to_all | solution.py:12
  45.6 0.8 reshape.58
  46.4 0.1 copy.62
  46.6 0.0 copy-start.4
  46.6 0.9 copy-done.4
  47.4 0.6 fusion.7
  48.0 1.0 copy.50
  49.1 3.9 %all-to-all-start.1 = ((bf16[8,64,768]{2,1,0:T(8,128)(2,1)}), bf16[8,64,768]{2,1,0:T(8,128)(2,1)S(1)}, u32[]{:S(2)}, u32[]{:S(2)}) async-start(bf16[8,64,768]{2,1,0:T(8,128)(2,1)} %copy.50), calls=%async_computation.1 | async-start | bytes 1572864 | tf_op jit(solution)/shard_map/all_to_all | solution.py:16
  52.9 1.4 copy.46
  54.3 0.0 copy-done.7
  54.4 1.2 copy.52
  55.5 17.6 %all-to-all-done.1 = bf16[8,64,768]{2,1,0:T(8,128)(2,1)S(1)} async-done(((bf16[8,64,768]{2,1,0:T(8,128)(2,1)}), bf16[8,64,768]{2,1,0:T(8,128)(2,1)S(1)}, u32[]{:S(2)}, u32[]{:S(2)}) %all-to-all-start.1) | async-done | bytes 786464 | tf_op jit(solution)/shard_map/all_to_all | solution.py:16
  73.1 0.9 copy-done.3
  74.0 1.2 bitcast_convert_fusion
  75.2 1.6 copy.51
  76.8 3.4 %fusion.6 = (bf16[1,512,768]{1,2,0:T(8,128)(2,1)}, bf16[1,512,768]{1,2,0:T(8,128)(2,1)}) fusion(bf16[1,512,768]{1,2,0:T(8,128)(2,1)} %copy.52, bf16[1,512,768]{1,2,0:T(8,128)(2,1)S(1)} %copy.46, f32[1,512,768]{1,2,0:T(8,128)} %copy.51), kind=kLoop, calls=%fused_computation.10 | loop fusion | flops 3932160 | bytes 4718592 | tf_op jit(solution)/shard_map/convert_element_type | solution.py:17
  80.2 3.7 %copy.53 = bf16[1,512,768]{2,0,1:T(2,128)(2,1)S(1)} copy(bf16[1,512,768]{1,2,0:T(8,128)(2,1)} %get-tuple-element.20) | data formatting | bytes 1572864 | tf_op jit(solution)/shard_map/convert_element_type | solution.py:17
  84.0 6.3 %reduce.1 = bf16[512,768]{1,0:T(8,128)(2,1)} reduce(bf16[512,1,768]{2,1,0:T(2,128)(2,1)S(1)} %bitcast.40, bf16[]{:T(256)} %broadcast.12), dimensions={1}, to_apply=%bitcast.30.reduce_sub_computation | reduce | bytes 1572866
  90.3 2.2 %reshape.59 = bf16[8,2,24576]{2,1,0:T(2,128)(2,1)S(1)} reshape(bf16[512,768]{1,0:T(8,128)(2,1)} %reduce.1) | data formatting | bytes 1572864
  92.5 23.8 %all_to_all.42 = bf16[8,2,24576]{2,1,0:T(2,128)(2,1)} all-to-all(bf16[8,2,24576]{2,1,0:T(2,128)(2,1)S(1)} %reshape.59), channel_id=1, replica_groups=mesh['dp'=4,'seq'=8] {'seq'}, dimensions={0} | all-to-all | bytes 1572864 | tf_op jit(solution)/shard_map/all_to_all | solution.py:18
  116.3 4.1 %reshape.60 = bf16[512,1,768]{2,1,0:T(2,128)(2,1)S(1)} reshape(bf16[8,2,24576]{2,1,0:T(2,128)(2,1)} %all_to_all.42) | data formatting | bytes 1572864
  120.4 0.1 copy.63
  120.5 0.6 fusion.8
  121.1 0.3 copy-done.6
  121.4 1.0 copy.56
  122.5 4.3 %all-to-all-start.3 = ((bf16[8,64,768]{2,1,0:T(8,128)(2,1)}), bf16[8,64,768]{2,1,0:T(8,128)(2,1)}, u32[]{:S(2)}, u32[]{:S(2)}) async-start(bf16[8,64,768]{2,1,0:T(8,128)(2,1)} %copy.56), calls=%async_computation.3 | async-start | bytes 1572864 | tf_op jit(solution)/shard_map/all_to_all | solution.py:23
  126.8 0.0 all-reduce.2.cloned.1.call-start
  126.9 1.2 copy.59
  128.0 2.1 %convolution_convert_fusion.4 = bf16[64,8,8]{2,1,0:T(8,128)(2,1)S(1)} fusion(bf16[8,64,768]{2,1,0:T(8,128)(2,1)} %bitcast.47, bf16[8,64,768]{2,1,0:T(8,128)(2,1)S(1)} %bitcast.45), kind=kOutput, calls=%fused_computation.19 | convolution fusion | flops 6295552 | bytes 1581056 | tf_op jit(solution)/shard_map/arc,brc->rab/dot_general | solution.py:22
  130.1 12.4 %psum.15 = bf16[64,8,8]{2,1,0:T(8,128)(2,1)S(1)} all-reduce(bf16[64,8,8]{2,1,0:T(8,128)(2,1)S(1)} %convolution_convert_fusion.4), channel_id=1, replica_groups=mesh['dp'=4,'seq'=8] {'dp'}, use_global_device_ids=true, to_apply=%region_1.0 | all-reduce | flops 4096 | bytes 16384 | tf_op jit(solution)/shard_map/psum | solution.py:28
  142.5 0.7 copy.61
  143.2 3.0 %all-to-all-done.3 = bf16[8,64,768]{2,1,0:T(8,128)(2,1)} async-done(((bf16[8,64,768]{2,1,0:T(8,128)(2,1)}), bf16[8,64,768]{2,1,0:T(8,128)(2,1)}, u32[]{:S(2)}, u32[]{:S(2)}) %all-to-all-start.3) | async-done | bytes 786464 | tf_op jit(solution)/shard_map/all_to_all | solution.py:23
  146.2 2.8 %fusion.10 = bf16[1,512,512]{2,1,0:T(8,128)(2,1)} fusion(bf16[512,768]{1,0:T(8,128)(2,1)} %bitcast.6, bf16[1,512,768]{2,1,0:T(8,128)(2,1)} %param.4), kind=kOutput, calls=%fused_computation.18 | convolution fusion | flops 402915328 | bytes 2097152 | tf_op jit(solution)/shard_map/bsc,brc->bsr/dot_general | solution.py:25
  149.0 0.0 all-reduce.2.cloned.1.call-update
  149.0 3.2 %fusion.5 = bf16[1,512,768]{1,2,0:T(8,128)(2,1)} fusion(bf16[1,512,768]{1,2,0:T(8,128)(2,1)} %copy.52, bf16[512,768]{1,0:T(8,128)(2,1)} %bitcast.6, f32[1,512,768]{1,2,0:T(8,128)S(1)} %copy-done.1, bf16[1,512,512]{2,1,0:T(8,128)(2,1)S(1)} %copy-done, bf16[1,512,768]{1,2,0:T(8,128)(2,1)S(1)} %copy.46), kind=kOutput, calls=%fused_computation.9 | convolution fusion | flops 407371776 | bytes 5242880 | tf_op jit(solution)/shard_map/bsr,bsc->brc/dot_general | solution.py:24
  152.3 2.3 %copy.60 = bf16[1,512,768]{2,1,0:T(8,128)(2,1)} copy(bf16[1,512,768]{1,2,0:T(8,128)(2,1)} %fusion.5) | data formatting | bytes 1572864
  154.6 26.8 %all-reduce.2.cloned.1.call-done = bf16[1,512,512]{2,1,0:T(8,128)(2,1)} async-done(((bf16[1,512,512]{2,1,0:T(8,128)(2,1)}), bf16[1,512,512]{2,1,0:T(8,128)(2,1)}) %all-reduce.2.cloned.1.call-update) | async-done | bytes 524304 | tf_op jit(solution)/shard_map/psum | solution.py:27
  181.3 1.9 copy.75
  (10 shorter events, 0.0 us)
Async XLA Ops:
  7.2 1.0 copy-start
  17.1 8.4 %copy-start.8 = (bf16[64,8,8]{0,2,1:T(8,128)(2,1)S(1)}, bf16[64,8,8]{0,2,1:T(8,128)(2,1)}, u32[]{:S(2)}) copy-start(bf16[64,8,8]{0,2,1:T(8,128)(2,1)} %param.6) | copy-start | bytes 24580
  18.2 27.5 %all-to-all-start = ((bf16[8,2,24576]{2,1,0:T(2,128)(2,1)}), bf16[8,2,24576]{2,1,0:T(2,128)(2,1)S(1)}, u32[]{:S(2)}, u32[]{:S(2)}) async-start(bf16[8,2,24576]{2,1,0:T(2,128)(2,1)} %reshape.57), calls=%async_computation | async-start | bytes 1572864 | tf_op jit(solution)/shard_map/all_to_all | solution.py:12
  46.6 0.9 copy-start.4
  49.1 5.3 %copy-start.7 = (bf16[1,512,768]{2,1,0:T(8,128)(2,1)S(1)}, bf16[1,512,768]{2,1,0:T(8,128)(2,1)}, u32[]{:S(2)}) copy-start(bf16[1,512,768]{2,1,0:T(8,128)(2,1)} %param.7) | copy-start | bytes 2359300
  49.1 24.0 %all-to-all-start.1 = ((bf16[8,64,768]{2,1,0:T(8,128)(2,1)}), bf16[8,64,768]{2,1,0:T(8,128)(2,1)S(1)}, u32[]{:S(2)}, u32[]{:S(2)}) async-start(bf16[8,64,768]{2,1,0:T(8,128)(2,1)} %copy.50), calls=%async_computation.1 | async-start | bytes 1572864 | tf_op jit(solution)/shard_map/all_to_all | solution.py:16
  73.1 0.9 copy-start.3
  120.5 0.9 copy-start.6
  121.4 5.4 %copy-start.2 = (bf16[1,512,768]{1,2,0:T(8,128)(2,1)S(1)}, bf16[1,512,768]{1,2,0:T(8,128)(2,1)}, u32[]{:S(2)}) copy-start(bf16[1,512,768]{1,2,0:T(8,128)(2,1)} %get-tuple-element.21) | copy-start | bytes 2359300
  122.5 5.6 %copy-start.5 = (bf16[1,512,768]{2,1,0:T(8,128)(2,1)S(1)}, bf16[1,512,768]{2,1,0:T(8,128)(2,1)}, u32[]{:S(2)}) copy-start(bf16[1,512,768]{2,1,0:T(8,128)(2,1)} %copy-done.4) | copy-start | bytes 2359300
  122.5 23.8 %all-to-all-start.3 = ((bf16[8,64,768]{2,1,0:T(8,128)(2,1)}), bf16[8,64,768]{2,1,0:T(8,128)(2,1)}, u32[]{:S(2)}, u32[]{:S(2)}) async-start(bf16[8,64,768]{2,1,0:T(8,128)(2,1)} %copy.56), calls=%async_computation.3 | async-start | bytes 1572864 | tf_op jit(solution)/shard_map/all_to_all | solution.py:23
  126.8 54.5 %all-reduce.2.cloned.1.call-start = ((), (), s32[]{:S(2)}) async-start(), calls=%async_computation.4 | async-start | bytes 1048576 | tf_op jit(solution)/shard_map/psum | solution.py:27
  142.5 6.5 %copy-start.1 = (f32[1,512,768]{1,2,0:T(8,128)S(1)}, f32[1,512,768]{1,2,0:T(8,128)}, u32[]{:S(2)}) copy-start(f32[1,512,768]{1,2,0:T(8,128)} %copy.51) | copy-start | bytes 4718596
Sparse Core Ops, SparseCore 0:
  149.2 32.1 all-reduce.1
where the time goes:
time: 191 us; the launch traced here: 190 us
  waiting for transfers between devices  67.4 us (35%)
  blocking collectives  36.1 us (19%)
  local copies, waits for them, and re-layouts  29.5 us (15%)
  other arithmetic  16.4 us (9%)
  starting transfers between devices  15.5 us (8%)
  between operations  14.2 us (7%)
  matrix products  10.9 us (6%)
    psum x1, waiting for transfers between devices, local(): lax.psum(block_part.astype(jnp.bfloat16), 'dp').astype(jnp.float32)  26.8 us
    all_to_all x1, blocking collectives, local(): dz_cols = lax.all_to_all(dz, 'seq', split_axis=1, concat_axis=0, tiled=True)  23.8 us
    unnamed x32, local copies, waits for them, and re-layouts  20.9 us
    all_to_all x1, waiting for transfers between devices, local(): h_cols = lax.all_to_all(h, 'seq', split_axis=1, concat_axis=0, tiled=True)  20 us
    all_to_all x1, waiting for transfers between devices, local(): z = lax.all_to_all(z_cols, 'seq', split_axis=0, concat_axis=1, tiled=True)  17.6 us
    psum x1, blocking collectives, local(): lax.psum(cross_part.astype(jnp.bfloat16), 'dp').astype(jnp.float32)  12.4 us
    unnamed x2, other arithmetic  11.7 us
    all_to_all x1, starting transfers between devices, local(): h_cols = lax.all_to_all(h, 'seq', split_axis=1, concat_axis=0, tiled=True)  7.28 us
  transfers between devices with their start and end apart: 4, of which 4 were waited for; matrix products, arithmetic and copies ran while one was open for 6% of the time, Pallas kernels for 0%

commit v1 on v0

--- a/solution.py
+++ b/solution.py
@@ -23,8 +23,9 @@
     dh = lax.all_to_all(dh_cols, "seq", split_axis=0, concat_axis=1, tiled=True)
     dv = jnp.einsum("bsr,bsc->brc", block_mix, dh, preferred_element_type=jnp.float32)
     block_part = jnp.einsum("bsc,brc->bsr", dh, inputs, preferred_element_type=jnp.float32)
+    _convert_patches = lambda frame_in: jnp.sum(lax.all_gather(frame_in, axis_name="dp"), axis=0)
     block_sum, cross_sum = (
-        lax.psum(block_part.astype(jnp.bfloat16), "dp").astype(jnp.float32),
+        _convert_patches(block_part.astype(jnp.bfloat16)).astype(jnp.float32),
         lax.psum(cross_part.astype(jnp.bfloat16), "dp").astype(jnp.float32),
     )
     zf = z.astype(jnp.float32)

time: 191 us -> 181 us (0.948)
  waiting for transfers between devices: 67.4 us -> 37.6 us
  blocking collectives: 36.1 us -> 60.4 us
  starting transfers between devices: 15.5 us -> 11.2 us
  other arithmetic: 16.4 us -> 19.3 us
  local copies, waits for them, and re-layouts: 29.5 us -> 27.4 us
    psum x1 -> x0, waiting for transfers between devices: 26.8 us -> none  [local(): lax.psum(block_part.astype(jnp.bfloat16), 'dp').astype(jnp.float32)]
    all_to_all x0 -> x1, blocking collectives: none -> 23.2 us  [local(): dh = lax.all_to_all(dh_cols, 'seq', split_axis=0, concat_axis=1, tiled=True)]
    all_to_all x1 -> x0, starting transfers between devices: 4.34 us -> none  [local(): dh = lax.all_to_all(dh_cols, 'seq', split_axis=0, concat_axis=1, tiled=True)]
    all_to_all x1 -> x0, waiting for transfers between devices: 3.01 us -> none  [local(): dh = lax.all_to_all(dh_cols, 'seq', split_axis=0, concat_axis=1, tiled=True)]
    reduce_sum x0 -> x1, other arithmetic: none -> 2.85 us  [local(): jnp.sum(lax.all_gather(frame_in, axis_name='dp'), axis=0)]
    unnamed x32 -> x33, local copies, waits for them, and re-layouts: 20.9 us -> 19.7 us
  transfers between devices with their start and end apart: 4 -> 3, of which waited for: 4 -> 2; matrix products, arithmetic and copies ran while one was open for 6% -> 7% of each run, Pallas kernels for 0% -> 0%
where the time goes in v1:
time: 181 us; the launch traced here: 180 us
  blocking collectives  60.4 us (33%)
  waiting for transfers between devices  37.6 us (21%)
  local copies, waits for them, and re-layouts  27.4 us (15%)
  other arithmetic  19.3 us (11%)
  between operations  14.2 us (8%)
  starting transfers between devices  11.2 us (6%)
  matrix products  9.93 us (5%)
    all_to_all x1, blocking collectives, local(): dz_cols = lax.all_to_all(dz, 'seq', split_axis=1, concat_axis=0, tiled=True)  23.7 us
    all_to_all x1, blocking collectives, local(): dh = lax.all_to_all(dh_cols, 'seq', split_axis=0, concat_axis=1, tiled=True)  23.2 us
    all_to_all x1, waiting for transfers between devices, local(): h_cols = lax.all_to_all(h, 'seq', split_axis=1, concat_axis=0, tiled=True)  20 us
    unnamed x33, local copies, waits for them, and re-layouts  19.7 us
    all_to_all x1, waiting for transfers between devices, local(): z = lax.all_to_all(z_cols, 'seq', split_axis=0, concat_axis=1, tiled=True)  17.6 us
    psum x1, blocking collectives, local(): lax.psum(cross_part.astype(jnp.bfloat16), 'dp').astype(jnp.float32)  13.4 us
    unnamed x2, other arithmetic  11.7 us
    all_to_all x1, starting transfers between devices, local(): h_cols = lax.all_to_all(h, 'seq', split_axis=1, concat_axis=0, tiled=True)  7.28 us
  transfers between devices with their start and end apart: 3, of which 2 were waited for; matrix products, arithmetic and copies ran while one was open for 7% of the time, Pallas kernels for 0%

profile of v1, /device:TPU:0, one launch (start us, length us, event | category | flops | bytes accessed | tf_op | source)
XLA Modules:
  0.0 180.0 jit_solution(18068911477165368625)
XLA Ops:
  7.2 0.0 copy-start
  7.2 1.0 copy-done
  8.2 1.7 fusion.9
  9.9 1.2 copy.73
  11.1 0.5 broadcast.12
  11.7 5.4 %reduce.3 = bf16[512,768]{1,0:T(8,128)(2,1)S(1)} reduce(bf16[512,1,768]{2,1,0:T(2,128)(2,1)S(1)} %bitcast.39, bf16[]{:T(256)} %broadcast.12), dimensions={1}, to_apply=%bitcast.37.reduce_sub_computation | reduce | bytes 1572866
  17.1 0.0 copy-start.9
  17.1 1.1 reshape.61
  18.2 7.3 %all-to-all-start = ((bf16[8,2,24576]{2,1,0:T(2,128)(2,1)}), bf16[8,2,24576]{2,1,0:T(2,128)(2,1)S(1)}, u32[]{:S(2)}, u32[]{:S(2)}) async-start(bf16[8,2,24576]{2,1,0:T(2,128)(2,1)} %reshape.61), calls=%async_computation | async-start | bytes 1572864 | tf_op jit(solution)/shard_map/all_to_all | solution.py:12
  25.4 0.1 copy.55
  25.6 20.0 %all-to-all-done = bf16[8,2,24576]{2,1,0:T(2,128)(2,1)S(1)} async-done(((bf16[8,2,24576]{2,1,0:T(2,128)(2,1)}), bf16[8,2,24576]{2,1,0:T(2,128)(2,1)S(1)}, u32[]{:S(2)}, u32[]{:S(2)}) %all-to-all-start) | async-done | bytes 786464 | tf_op jit(solution)/shard_map/all_to_all | solution.py:12
  45.6 0.8 reshape.62
  46.4 0.1 copy.62
  46.6 0.0 copy-start.4
  46.6 0.9 copy-done.4
  47.5 0.6 fusion.7
  48.0 1.0 copy.50
  49.1 3.7 %all-to-all-start.1 = ((bf16[8,64,768]{2,1,0:T(8,128)(2,1)}), bf16[8,64,768]{2,1,0:T(8,128)(2,1)S(1)}, u32[]{:S(2)}, u32[]{:S(2)}) async-start(bf16[8,64,768]{2,1,0:T(8,128)(2,1)} %copy.50), calls=%async_computation.1 | async-start | bytes 1572864 | tf_op jit(solution)/shard_map/all_to_all | solution.py:16
  52.8 0.2 all-gather.3.cloned.1.call-start
  53.0 1.4 copy.46
  54.4 0.0 copy-done.6
  54.4 1.2 copy.52
  55.6 17.6 %all-to-all-done.1 = bf16[8,64,768]{2,1,0:T(8,128)(2,1)S(1)} async-done(((bf16[8,64,768]{2,1,0:T(8,128)(2,1)}), bf16[8,64,768]{2,1,0:T(8,128)(2,1)S(1)}, u32[]{:S(2)}, u32[]{:S(2)}) %all-to-all-start.1) | async-done | bytes 786464 | tf_op jit(solution)/shard_map/all_to_all | solution.py:16
  73.1 0.9 copy-done.3
  74.0 1.2 bitcast_convert_fusion
  75.3 1.6 copy.51
  76.9 3.4 %fusion.6 = (bf16[1,512,768]{1,2,0:T(8,128)(2,1)}, bf16[1,512,768]{1,2,0:T(8,128)(2,1)}) fusion(bf16[1,512,768]{1,2,0:T(8,128)(2,1)} %copy.52, bf16[1,512,768]{1,2,0:T(8,128)(2,1)S(1)} %copy.46, f32[1,512,768]{1,2,0:T(8,128)} %copy.51), kind=kLoop, calls=%fused_computation.10 | loop fusion | flops 3932160 | bytes 4718592 | tf_op jit(solution)/shard_map/convert_element_type | solution.py:17
  80.3 3.7 %copy.53 = bf16[1,512,768]{2,0,1:T(2,128)(2,1)S(1)} copy(bf16[1,512,768]{1,2,0:T(8,128)(2,1)} %get-tuple-element.20) | data formatting | bytes 1572864 | tf_op jit(solution)/shard_map/convert_element_type | solution.py:17
  84.1 6.3 %reduce.4 = bf16[512,768]{1,0:T(8,128)(2,1)} reduce(bf16[512,1,768]{2,1,0:T(2,128)(2,1)S(1)} %bitcast.40, bf16[]{:T(256)} %broadcast.12), dimensions={1}, to_apply=%bitcast.30.reduce_sub_computation | reduce | bytes 1572866
  90.4 2.2 %reshape.63 = bf16[8,2,24576]{2,1,0:T(2,128)(2,1)S(1)} reshape(bf16[512,768]{1,0:T(8,128)(2,1)} %reduce.4) | data formatting | bytes 1572864
  92.6 23.7 %all_to_all.42 = bf16[8,2,24576]{2,1,0:T(2,128)(2,1)} all-to-all(bf16[8,2,24576]{2,1,0:T(2,128)(2,1)S(1)} %reshape.63), channel_id=1, replica_groups=mesh['dp'=4,'seq'=8] {'seq'}, dimensions={0} | all-to-all | bytes 1572864 | tf_op jit(solution)/shard_map/all_to_all | solution.py:18
  116.4 4.1 %reshape.64 = bf16[512,1,768]{2,1,0:T(2,128)(2,1)S(1)} reshape(bf16[8,2,24576]{2,1,0:T(2,128)(2,1)} %all_to_all.42) | data formatting | bytes 1572864
  120.5 0.1 copy.63
  120.6 0.6 fusion.8
  121.2 0.0 copy-start.7
  121.2 0.1 copy.56
  121.3 0.2 copy-done.5
  121.5 23.2 %all_to_all.43 = bf16[8,64,768]{2,1,0:T(8,128)(2,1)S(1)} all-to-all(bf16[8,64,768]{2,1,0:T(8,128)(2,1)S(1)} %copy.56), channel_id=1, replica_groups=mesh['dp'=4,'seq'=8] {'seq'}, dimensions={0} | all-to-all | bytes 1572864 | tf_op jit(solution)/shard_map/all_to_all | solution.py:23
  144.7 0.9 copy-done.8
  145.6 1.4 convolution_convert_fusion.3
  147.0 0.0 all-gather.3.cloned.1.call-update
  147.0 1.2 copy.59
  148.2 2.4 %convolution_convert_fusion.4 = bf16[64,8,8]{2,1,0:T(8,128)(2,1)S(1)} fusion(bf16[8,64,768]{2,1,0:T(8,128)(2,1)} %bitcast.47, bf16[8,64,768]{2,1,0:T(8,128)(2,1)} %bitcast.45), kind=kOutput, calls=%fused_computation.18 | convolution fusion | flops 6295552 | bytes 1581056 | tf_op jit(solution)/shard_map/arc,brc->rab/dot_general | solution.py:22
  150.6 13.4 %psum.7 = bf16[64,8,8]{2,1,0:T(8,128)(2,1)S(1)} all-reduce(bf16[64,8,8]{2,1,0:T(8,128)(2,1)S(1)} %convolution_convert_fusion.4), channel_id=1, replica_groups=mesh['dp'=4,'seq'=8] {'dp'}, use_global_device_ids=true, to_apply=%region_1.0 | all-reduce | flops 4096 | bytes 16384 | tf_op jit(solution)/shard_map/psum | solution.py:29
  164.0 0.7 copy.61
  164.7 3.3 %fusion.5 = bf16[1,512,768]{1,2,0:T(8,128)(2,1)} fusion(bf16[1,512,768]{1,2,0:T(8,128)(2,1)} %copy.52, bf16[512,768]{1,0:T(8,128)(2,1)} %bitcast.50, f32[1,512,768]{1,2,0:T(8,128)S(1)} %copy-done.1, bf16[1,512,512]{2,1,0:T(8,128)(2,1)S(1)} %copy-done, bf16[1,512,768]{1,2,0:T(8,128)(2,1)S(1)} %copy.46), kind=kOutput, calls=%fused_computation.9 | convolution fusion | flops 407371776 | bytes 5242880 | tf_op jit(solution)/shard_map/bsr,bsc->brc/dot_general | solution.py:24
  168.0 2.3 %copy.60 = bf16[1,512,768]{2,1,0:T(8,128)(2,1)} copy(bf16[1,512,768]{1,2,0:T(8,128)(2,1)} %fusion.5) | data formatting | bytes 1572864
  170.3 2.9 %reduce.2 = bf16[512,512]{1,0:T(8,128)(2,1)} reduce(bf16[4,512,512]{2,1,0:T(8,128)(2,1)} %bitcast.48, bf16[]{:T(256)} %constant.4.clone.1), dimensions={0}, to_apply=%region_0.0 | reduce | flops 786432 | bytes 2621442 | tf_op jit(solution)/shard_map/reduce_sum | solution.py:26
  (11 shorter events, 0.0 us)
Async XLA Ops:
  7.2 1.0 copy-start
  17.1 8.4 %copy-start.9 = (bf16[64,8,8]{0,2,1:T(8,128)(2,1)S(1)}, bf16[64,8,8]{0,2,1:T(8,128)(2,1)}, u32[]{:S(2)}) copy-start(bf16[64,8,8]{0,2,1:T(8,128)(2,1)} %param.6) | copy-start | bytes 24580
  18.2 27.5 %all-to-all-start = ((bf16[8,2,24576]{2,1,0:T(2,128)(2,1)}), bf16[8,2,24576]{2,1,0:T(2,128)(2,1)S(1)}, u32[]{:S(2)}, u32[]{:S(2)}) async-start(bf16[8,2,24576]{2,1,0:T(2,128)(2,1)} %reshape.61), calls=%async_computation | async-start | bytes 1572864 | tf_op jit(solution)/shard_map/all_to_all | solution.py:12
  46.6 0.9 copy-start.4
  49.1 5.3 %copy-start.6 = (bf16[1,512,768]{2,1,0:T(8,128)(2,1)S(1)}, bf16[1,512,768]{2,1,0:T(8,128)(2,1)}, u32[]{:S(2)}) copy-start(bf16[1,512,768]{2,1,0:T(8,128)(2,1)} %param.7) | copy-start | bytes 2359300
  49.1 24.1 %all-to-all-start.1 = ((bf16[8,64,768]{2,1,0:T(8,128)(2,1)}), bf16[8,64,768]{2,1,0:T(8,128)(2,1)S(1)}, u32[]{:S(2)}, u32[]{:S(2)}) async-start(bf16[8,64,768]{2,1,0:T(8,128)(2,1)} %copy.50), calls=%async_computation.1 | async-start | bytes 1572864 | tf_op jit(solution)/shard_map/all_to_all | solution.py:16
  52.8 117.5 %all-gather.3.cloned.1.call-start = ((), (), s32[]{:S(2)}) async-start(), calls=%async_computation.4 | async-start | bytes 2621440 | tf_op jit(solution)/shard_map/all_gather | solution.py:26
  73.1 0.9 copy-start.3
  120.6 0.9 copy-start.5
  121.2 24.4 %copy-start.7 = (bf16[1,512,768]{2,1,0:T(8,128)(2,1)S(1)}, bf16[1,512,768]{2,1,0:T(8,128)(2,1)}, u32[]{:S(2)}) copy-start(bf16[1,512,768]{2,1,0:T(8,128)(2,1)} %param.4) | copy-start | bytes 2359300
  144.7 0.9 copy-start.8
  144.7 2.3 %copy-start.2 = (bf16[1,512,768]{1,2,0:T(8,128)(2,1)S(1)}, bf16[1,512,768]{1,2,0:T(8,128)(2,1)}, u32[]{:S(2)}) copy-start(bf16[1,512,768]{1,2,0:T(8,128)(2,1)} %get-tuple-element.21) | copy-start | bytes 2359300
  148.2 16.6 %copy-start.1 = (f32[1,512,768]{1,2,0:T(8,128)S(1)}, f32[1,512,768]{1,2,0:T(8,128)}, u32[]{:S(2)}) copy-start(f32[1,512,768]{1,2,0:T(8,128)} %copy.51) | copy-start | bytes 4718596
Sparse Core Ops, SparseCore 0:
  147.1 22.9 all-gather.2
